TPU v7x, 32 devices: a whole 2x2x4 slice. The times are simulated.
32 devices in a mesh: mode: 4 (over z), space: 8 (over y, x, core).
Axes of the slice: x: 2, y: 2, z: 4, core: 2. Of those that a mesh axis runs over, the one named last changes fastest.
Arguments:
- traces: float32 [120, 24576], P('mode', 'space'), may hold values from -6 to 6
- elem_mats: float32 [5, 36, 8192], P(None, None, 'space'), may hold values from -1.8 to 1.8
- face_links: int32 [6, 8192], P(None, 'space'), may hold values from 0 to 4095
- pair_modes: int32 [2, 1440], replicated, may hold values from 0 to 119
- pair_terms: int32 [1440], replicated, may hold values from 0 to 3
- pair_values: float32 [1440], replicated, may hold values from -3 to 3
Outputs:
- applied: float32 [120, 24576], P('mode', 'space')
Inputs may be any that keep to these rules, and one draw needn't show every extreme that they name: `face_links`: indices into an element's subdomain's 3072 faces preceded and followed by 512 faces of the neighbouring subdomains.
All inputs are finite; a program needn't handle non-finite values.
Results may differ from a plain program's by a relative error of at most 0.0001.
Values sent between devices are 32-bit elements; how exact they have to be, the bound alone decides.
A program may use at most 128 MiB of HBM per device.

v0:
```python
import functools

import jax
import jax.numpy as jnp
from jax import lax
from jax.experimental import pallas as pl
from jax.experimental.pallas import tpu as pltpu
from jax.sharding import PartitionSpec as P

HALO = 512
DIGIT = 256
BF = jnp.bfloat16


def coupling_rows(pair_modes, pair_terms, pair_values, rows, mode_count, term_count, first, pad_rows, pad_cols):
    groups = mode_count // rows
    row_key = jnp.where(
        (pair_modes[0] >= first) & (pair_modes[0] < first + rows),
        (pair_terms + 1) * pad_rows + pair_modes[0] - first,
        -1,
    )
    col_key = (pair_modes[1] // rows) * pad_cols + pair_modes[1] % rows
    row_ids = jnp.arange((term_count + 1) * pad_rows, dtype=jnp.int32)
    col_ids = jnp.arange(groups * pad_cols, dtype=jnp.int32)
    hits = (row_key[None, :] == row_ids[:, None]).astype(jnp.float32) * pair_values[None, :]
    cols = (col_key[:, None] == col_ids[None, :]).astype(jnp.float32)
    table = jnp.dot(hits, cols, precision=lax.Precision.HIGHEST)
    own = (first // rows) * pad_cols
    unit = (row_ids[:, None] + own == col_ids[None, :]) & (row_ids[:, None] < rows)
    return table + unit.astype(jnp.float32)


def split(value):
    high = value.astype(BF)
    return high, (value - high.astype(jnp.float32)).astype(BF)


def kernel(dims, x_ref, coupling_ref, mats_ref, links_ref, out_ref, low_ref, x2_ref, z_ref, v_ref, acc_ref):
    groups, rows, pad, terms, slots, elems, ext = dims
    tops = ext // DIGIT
    per_slot = elems // DIGIT
    chunks = slots * per_slot
    modes = groups * pad
    x2_ref[...] = jnp.zeros_like(x2_ref)
    for d in range(groups):
        for h in range(tops):
            high, low = split(x_ref[d, :, h * DIGIT : (h + 1) * DIGIT])
            base = h * modes + d * pad
            x2_ref[0, base : base + rows, :] = high
            x2_ref[1, base : base + rows, :] = low
    c_high, c_low = split(coupling_ref[...])

    @pl.loop(0, chunks)
    def _(c):
        links = links_ref[c]
        ids = lax.broadcasted_iota(jnp.int32, (DIGIT, DIGIT), 0)
        table = (ids == links % DIGIT).astype(jnp.float32).astype(BF)
        low_ref[c] = table
        found = jnp.dot(x2_ref[0], table, preferred_element_type=jnp.float32)
        found = found + jnp.dot(x2_ref[1], table, preferred_element_type=jnp.float32)
        tops_of = links // DIGIT
        g = jnp.zeros((modes, DIGIT), jnp.float32)
        for h in range(tops):
            g = jnp.where(tops_of == h, found[h * modes : (h + 1) * modes], g)
        g_high, g_low = split(g)
        z = jnp.dot(c_high, g_high, preferred_element_type=jnp.float32)
        z = z + jnp.dot(c_high, g_low, preferred_element_type=jnp.float32)
        z_ref[c] = z + jnp.dot(c_low, g_high, preferred_element_type=jnp.float32)

    acc_ref[...] = jnp.zeros_like(acc_ref)

    @pl.loop(0, slots)
    def _(a):
        for e in range(0, elems, 128):
            q, lane = e // DIGIT, e % DIGIT
            total = jnp.zeros((pad, 128), jnp.float32)
            for k in range(terms):
                for b in range(slots):
                    total = total + (
                        mats_ref[k, a, b : b + 1, e : e + 128]
                        * z_ref[b * per_slot + q, k * pad : (k + 1) * pad, lane : lane + 128]
                    )
            high, low = split(total)
            v_ref[a * per_slot + q, :pad, lane : lane + 128] = high
            v_ref[a * per_slot + q, pad:, lane : lane + 128] = low

    @pl.loop(0, chunks)
    def _(c):
        v = v_ref[c]
        tops_of = links_ref[c] // DIGIT
        parts = [v * (tops_of == h).astype(jnp.float32).astype(BF) for h in range(tops)]
        acc_ref[...] += lax.dot_general(
            jnp.concatenate(parts, axis=0),
            low_ref[c],
            (((1,), (1,)), ((), ())),
            preferred_element_type=jnp.float32,
        )

    for h in range(tops):
        base = 2 * pad * h
        total = acc_ref[base : base + pad, :] + acc_ref[base + pad : base + 2 * pad, :]
        out_ref[:, h * DIGIT : (h + 1) * DIGIT] = total[:rows]


def body(traces, elem_mats, face_links, pair_modes, pair_terms, pair_values):
    rows, faces = traces.shape
    terms = elem_mats.shape[0]
    slots, elems = face_links.shape
    groups, spaces = lax.axis_size("mode"), lax.axis_size("space")
    ext = faces + 2 * HALO
    pad = -(-rows // 16) * 16
    first = lax.axis_index("mode") * rows
    coupling = coupling_rows(
        pair_modes, pair_terms, pair_values, rows, rows * groups, terms - 1, first, pad, pad
    )
    up = [(i, i + 1) for i in range(spaces - 1)]
    down = [(i + 1, i) for i in range(spaces - 1)]
    before = lax.ppermute(traces[:, faces - HALO :], "space", up)
    after = lax.ppermute(traces[:, :HALO], "space", down)
    extended = jnp.concatenate([before, traces, after], axis=1)
    x = lax.all_gather(extended, "mode")
    dims = (groups, rows, pad, terms, slots, elems, ext)
    tops = ext // DIGIT
    chunks = slots * elems // DIGIT
    vmem = pl.BlockSpec(memory_space=pltpu.VMEM)
    out = pl.pallas_call(
        functools.partial(kernel, dims),
        out_shape=jax.ShapeDtypeStruct((rows, ext), jnp.float32),
        in_specs=[vmem] * 4,
        out_specs=vmem,
        scratch_shapes=[
            pltpu.VMEM((chunks, DIGIT, DIGIT), BF),
            pltpu.VMEM((2, tops * groups * pad, DIGIT), BF),
            pltpu.VMEM((chunks, terms * pad, DIGIT), jnp.float32),
            pltpu.VMEM((chunks, 2 * pad, DIGIT), BF),
            pltpu.VMEM((2 * pad * tops, DIGIT), jnp.float32),
        ],
        compiler_params=pltpu.CompilerParams(vmem_limit_bytes=48 * 1024 * 1024),
    )(x, coupling, elem_mats.reshape(terms, slots, slots, elems), face_links.reshape(chunks, 1, DIGIT))
    from_next = lax.ppermute(out[:, :HALO], "space", down)
    from_prev = lax.ppermute(out[:, HALO + faces :], "space", up)
    mid = out[:, HALO : HALO + faces]
    return jnp.concatenate(
        [mid[:, :HALO] + from_prev, mid[:, HALO : faces - HALO], mid[:, faces - HALO :] + from_next], axis=1
    )


def solution(mesh):
    return jax.shard_map(
        body,
        mesh=mesh,
        in_specs=(P("mode", "space"), P(None, None, "space"), P(None, "space"), P(), P(), P()),
        out_specs=P("mode", "space"),
        check_vma=False,
    )
```

profile of v0, /device:TPU:1, one launch (start us, length us, event | category | flops | bytes accessed | tf_op | source)
XLA Modules:
  0.0 122.3 jit_solution(6245088781447483442)
XLA Ops:
  6.5 0.0 all-gather.4.cloned.1.call-start
  6.6 1.0 fusion.9
  7.5 4.5 %collective-permute-start = (f32[30,512]{1,0:T(8,128)S(1)}, f32[30,512]{1,0:T(8,128)S(1)}, u32[]{:S(2)}, u32[]{:S(2)}) collective-permute-start(f32[30,512]{1,0:T(8,128)S(1)} %get-tuple-element.10), channel_id=1, source_target_pairs={{0,1},{1,2},{2,3},{3,4},{4,5},{5,6},{6,7},{8,9},{9,10},{10,11},{11... | collective-permute-start | bytes 184328 | tf_op jit(solution)/shard_map/ppermute | solution.py:118
  12.1 1.9 %collective-permute-start.1 = (f32[30,512]{1,0:T(8,128)S(1)}, f32[30,512]{1,0:T(8,128)S(1)}, u32[]{:S(2)}, u32[]{:S(2)}) collective-permute-start(f32[30,512]{1,0:T(8,128)S(1)} %get-tuple-element.11), channel_id=1, source_target_pairs={{1,0},{2,1},{3,2},{4,3},{5,4},{6,5},{7,6},{9,8},{10,9},{11,10},{12... | collective-permute-start | bytes 184328 | tf_op jit(solution)/shard_map/ppermute | solution.py:119
  14.0 0.0 collective-permute-done
  14.0 3.6 %collective-permute-done.1 = f32[30,512]{1,0:T(8,128)S(1)} collective-permute-done((f32[30,512]{1,0:T(8,128)S(1)}, f32[30,512]{1,0:T(8,128)S(1)}, u32[]{:S(2)}, u32[]{:S(2)}) %collective-permute-start.1) | collective-permute-done | bytes 61472 | tf_op jit(solution)/shard_map/ppermute | solution.py:119
  17.6 1.8 %maximum_bitcast_fusion = f32[1,30,4096]{2,1,0:T(8,128)} fusion(f32[30,512]{1,0:T(8,128)S(1)} %collective-permute-done.1, f32[30,3072]{1,0:T(8,128)} %param.6, f32[30,512]{1,0:T(8,128)S(1)} %collective-permute-done), kind=kLoop, calls=%fused_computation.4 | loop fusion | flops 245760 | bytes 983040
  19.5 0.0 all-gather.4.cloned.1.call-update
  19.5 0.8 reshape.50.links_ref
  20.3 0.0 copy-done.1
  20.3 0.1 reshape.49.mats_ref
  20.5 0.0 copy-done.2
  20.5 0.1 remainder_reduce_fusion
  20.6 0.0 copy-done.3
  20.6 0.0 copy-done.4
  20.6 0.8 convolution_add_fusion.coupling_ref
  21.5 44.8 %all-gather.4.cloned.1.call-done.x_ref = f32[4,30,4096]{2,1,0:T(8,128)} async-done(((f32[1,30,4096]{2,1,0:T(8,128)}), f32[4,30,4096]{2,1,0:T(8,128)}) %all-gather.4.cloned.1.call-update) | async-done | bytes 1966096 | tf_op jit(solution)/shard_map/all_gather | solution.py:121
  66.3 1.6 %copy-done = f32[4,30,4096]{2,1,0:T(8,128)S(1)} copy-done((f32[4,30,4096]{2,1,0:T(8,128)S(1)}, f32[4,30,4096]{2,1,0:T(8,128)}, u32[]{:S(2)}) %copy-start) | copy-done | bytes 1966104
  67.9 35.6 %shard_map.64 = f32[30,4096]{1,0:T(8,128)S(1)} custom-call(f32[4,30,4096]{2,1,0:T(8,128)S(1)} %copy-done, f32[160,128]{1,0:T(8,128)S(1)} %convolution_add_fusion.coupling_ref, f32[5,6,6,1024]{3,2,1,0:T(8,128)S(1)} %reshape.49.mats_ref, s32[24,1,256]{2,1,0:T(1,128)S(1)} %reshape.50.links_ref), custom_call_target="tpu_custom_call" | custom-call | tf_op jit(solution)/shard_map/pallas_call | solution.py:126
  103.5 3.7 %collective-permute-start.2 = (f32[30,512]{1,0:T(8,128)S(1)}, f32[30,512]{1,0:T(8,128)S(1)}, u32[]{:S(2)}, u32[]{:S(2)}) collective-permute-start(f32[30,512]{1,0:T(8,128)S(1)} %slice.44), channel_id=1, source_target_pairs={{0,1},{1,2},{2,3},{3,4},{4,5},{5,6},{6,7},{8,9},{9,10},{10,11},{11... | collective-permute-start | bytes 184328 | tf_op jit(solution)/shard_map/ppermute | solution.py:141
  107.1 1.3 %collective-permute-done.2 = f32[30,512]{1,0:T(8,128)S(1)} collective-permute-done((f32[30,512]{1,0:T(8,128)S(1)}, f32[30,512]{1,0:T(8,128)S(1)}, u32[]{:S(2)}, u32[]{:S(2)}) %collective-permute-start.2) | collective-permute-done | bytes 61472 | tf_op jit(solution)/shard_map/ppermute | solution.py:141
  108.5 1.9 %collective-permute-start.3 = (f32[30,512]{1,0:T(8,128)S(1)}, f32[30,512]{1,0:T(8,128)S(1)}, u32[]{:S(2)}, u32[]{:S(2)}) collective-permute-start(f32[30,512]{1,0:T(8,128)S(1)} %get-tuple-element.9), channel_id=1, source_target_pairs={{1,0},{2,1},{3,2},{4,3},{5,4},{6,5},{7,6},{9,8},{10,9},{11,10},{12... | collective-permute-start | bytes 184328 | tf_op jit(solution)/shard_map/ppermute | solution.py:140
  110.4 4.3 %collective-permute-done.3 = f32[30,512]{1,0:T(8,128)S(1)} collective-permute-done((f32[30,512]{1,0:T(8,128)S(1)}, f32[30,512]{1,0:T(8,128)S(1)}, u32[]{:S(2)}, u32[]{:S(2)}) %collective-permute-start.3) | collective-permute-done | bytes 61472 | tf_op jit(solution)/shard_map/ppermute | solution.py:140
  114.7 0.8 pad_maximum_fusion
  (13 shorter events, 0.1 us)
Async XLA Ops:
  6.5 13.8 %copy-start.1 = (f32[5,36,1024]{2,1,0:T(8,128)S(1)}, f32[5,36,1024]{2,1,0:T(8,128)}, u32[]{:S(2)}) copy-start(f32[5,36,1024]{2,1,0:T(8,128)} %param.7) | copy-start | bytes 2211844
  6.5 13.9 %copy-start.2 = (s32[2,1440]{1,0:T(2,128)S(1)}, s32[2,1440]{1,0:T(2,128)}, u32[]{:S(2)}) copy-start(s32[2,1440]{1,0:T(2,128)} %param.9) | copy-start | bytes 34564
  6.5 14.1 %copy-start.3 = (s32[1440]{0:T(1024)S(1)}, s32[1440]{0:T(1024)}, u32[]{:S(2)}) copy-start(s32[1440]{0:T(1024)} %param.10) | copy-start | bytes 17284
  6.5 14.1 %copy-start.4 = (f32[1440]{0:T(1024)S(1)}, f32[1440]{0:T(1024)}, u32[]{:S(2)}) copy-start(f32[1440]{0:T(1024)} %param.11) | copy-start | bytes 17284
  6.5 59.7 %all-gather.4.cloned.1.call-start = ((), (), s32[]{:S(2)}) async-start(), calls=%async_computation | async-start | bytes 2621440 | tf_op jit(solution)/shard_map/all_gather | solution.py:121
  7.5 6.4 %collective-permute-start = (f32[30,512]{1,0:T(8,128)S(1)}, f32[30,512]{1,0:T(8,128)S(1)}, u32[]{:S(2)}, u32[]{:S(2)}) collective-permute-start(f32[30,512]{1,0:T(8,128)S(1)} %get-tuple-element.10), channel_id=1, source_target_pairs={{0,1},{1,2},{2,3},{3,4},{4,5},{5,6},{6,7},{8,9},{9,10},{10,11},{11... | collective-permute-start | bytes 184328 | tf_op jit(solution)/shard_map/ppermute | solution.py:118
  12.1 5.6 %collective-permute-start.1 = (f32[30,512]{1,0:T(8,128)S(1)}, f32[30,512]{1,0:T(8,128)S(1)}, u32[]{:S(2)}, u32[]{:S(2)}) collective-permute-start(f32[30,512]{1,0:T(8,128)S(1)} %get-tuple-element.11), channel_id=1, source_target_pairs={{1,0},{2,1},{3,2},{4,3},{5,4},{6,5},{7,6},{9,8},{10,9},{11,10},{12... | collective-permute-start | bytes 184328 | tf_op jit(solution)/shard_map/ppermute | solution.py:119
  66.3 1.6 %copy-start = (f32[4,30,4096]{2,1,0:T(8,128)S(1)}, f32[4,30,4096]{2,1,0:T(8,128)}, u32[]{:S(2)}) copy-start(f32[4,30,4096]{2,1,0:T(8,128)} %all-gather.4.cloned.1.call-done.x_ref) | copy-start | bytes 5898244
  103.5 5.0 %collective-permute-start.2 = (f32[30,512]{1,0:T(8,128)S(1)}, f32[30,512]{1,0:T(8,128)S(1)}, u32[]{:S(2)}, u32[]{:S(2)}) collective-permute-start(f32[30,512]{1,0:T(8,128)S(1)} %slice.44), channel_id=1, source_target_pairs={{0,1},{1,2},{2,3},{3,4},{4,5},{5,6},{6,7},{8,9},{9,10},{10,11},{11... | collective-permute-start | bytes 184328 | tf_op jit(solution)/shard_map/ppermute | solution.py:141
  108.5 6.2 %collective-permute-start.3 = (f32[30,512]{1,0:T(8,128)S(1)}, f32[30,512]{1,0:T(8,128)S(1)}, u32[]{:S(2)}, u32[]{:S(2)}) collective-permute-start(f32[30,512]{1,0:T(8,128)S(1)} %get-tuple-element.9), channel_id=1, source_target_pairs={{1,0},{2,1},{3,2},{4,3},{5,4},{6,5},{7,6},{9,8},{10,9},{11,10},{12... | collective-permute-start | bytes 184328 | tf_op jit(solution)/shard_map/ppermute | solution.py:140
Sparse Core Ops, SparseCore 0:
  19.6 46.6 all-gather.3
where the time goes:
time: 123 us; the launch traced here: 122 us
  waiting for transfers between devices  54 us (44%)
  Pallas kernels  35.6 us (29%)
  between operations  13.6 us (11%)
  starting transfers between devices  12 us (10%)
  local copies, waits for them, and re-layouts  3.47 us (3%)
  other arithmetic  2.76 us (2%)
    all_gather x1, waiting for transfers between devices, body(): x = lax.all_gather(extended, 'mode')  44.8 us
    pallas_call x1, Pallas kernels, body(): pl.pallas_call(functools.partial(kernel, dims), out_shape=jax.ShapeDtypeS...  35.6 us
    ppermute x1, starting transfers between devices, body(): before = lax.ppermute(traces[:, faces - HALO:], 'space', up)  4.51 us
    ppermute x1, waiting for transfers between devices, body(): from_next = lax.ppermute(out[:, :HALO], 'space', down)  4.25 us
    ppermute x1, starting transfers between devices, body(): from_prev = lax.ppermute(out[:, HALO + faces:], 'space', up)  3.66 us
    ppermute x1, waiting for transfers between devices, body(): after = lax.ppermute(traces[:, :HALO], 'space', down)  3.65 us
  transfers between devices with their start and end apart: 5, of which 4 were waited for; matrix products, arithmetic and copies ran while one was open for 2% of the time, Pallas kernels for 0%

commit v1 on v0

--- a/solution.py
+++ b/solution.py
@@ -19,14 +19,13 @@
         (pair_terms + 1) * pad_rows + pair_modes[0] - first,
         -1,
     )
-    col_key = (pair_modes[1] // rows) * pad_cols + pair_modes[1] % rows
+    col_key = ((pair_modes[1] // rows - first // rows + groups) % groups) * pad_cols + pair_modes[1] % rows
     row_ids = jnp.arange((term_count + 1) * pad_rows, dtype=jnp.int32)
     col_ids = jnp.arange(groups * pad_cols, dtype=jnp.int32)
     hits = (row_key[None, :] == row_ids[:, None]).astype(jnp.float32) * pair_values[None, :]
     cols = (col_key[:, None] == col_ids[None, :]).astype(jnp.float32)
     table = jnp.dot(hits, cols, precision=lax.Precision.HIGHEST)
-    own = (first // rows) * pad_cols
-    unit = (row_ids[:, None] + own == col_ids[None, :]) & (row_ids[:, None] < rows)
+    unit = (row_ids[:, None] == col_ids[None, :]) & (row_ids[:, None] < rows)
     return table + unit.astype(jnp.float32)
 
 
@@ -35,7 +34,13 @@
     return high, (value - high.astype(jnp.float32)).astype(BF)
 
 
-def kernel(dims, x_ref, coupling_ref, mats_ref, links_ref, out_ref, low_ref, x2_ref, z_ref, v_ref, acc_ref):
+def kernel(dims, own_ref, *refs):
+    groups = dims[0]
+    lower, upper = refs[: groups - 1], refs[groups - 1 : 2 * groups - 2]
+    compute(dims, own_ref, lower, upper, *refs[2 * groups - 2 :])
+
+
+def compute(dims, own_ref, lower, upper, coupling_ref, mats_ref, links_ref, out_ref, low_ref, x2_ref, z_ref, v_ref, acc_ref):
     groups, rows, pad, terms, slots, elems, ext = dims
     tops = ext // DIGIT
     per_slot = elems // DIGIT
@@ -44,7 +49,9 @@
     x2_ref[...] = jnp.zeros_like(x2_ref)
     for d in range(groups):
         for h in range(tops):
-            high, low = split(x_ref[d, :, h * DIGIT : (h + 1) * DIGIT])
+            at = slice(h * DIGIT, (h + 1) * DIGIT)
+            block = own_ref[:, at] if d == 0 else upper[d - 1][:, at] + lower[groups - d - 1][:, at]
+            high, low = split(block)
             base = h * modes + d * pad
             x2_ref[0, base : base + rows, :] = high
             x2_ref[1, base : base + rows, :] = low
@@ -118,7 +125,12 @@
     before = lax.ppermute(traces[:, faces - HALO :], "space", up)
     after = lax.ppermute(traces[:, :HALO], "space", down)
     extended = jnp.concatenate([before, traces, after], axis=1)
-    x = lax.all_gather(extended, "mode")
+    lower, upper = [extended], [extended]
+    right = [(i, i + 1) for i in range(groups - 1)]
+    left = [(i + 1, i) for i in range(groups - 1)]
+    for _ in range(groups - 1):
+        lower.append(lax.ppermute(lower[-1], "mode", right))
+        upper.append(lax.ppermute(upper[-1], "mode", left))
     dims = (groups, rows, pad, terms, slots, elems, ext)
     tops = ext // DIGIT
     chunks = slots * elems // DIGIT
@@ -126,7 +138,7 @@
     out = pl.pallas_call(
         functools.partial(kernel, dims),
         out_shape=jax.ShapeDtypeStruct((rows, ext), jnp.float32),
-        in_specs=[vmem] * 4,
+        in_specs=[vmem] * (2 * groups + 2),
         out_specs=vmem,
         scratch_shapes=[
             pltpu.VMEM((chunks, DIGIT, DIGIT), BF),
@@ -136,7 +148,7 @@
             pltpu.VMEM((2 * pad * tops, DIGIT), jnp.float32),
         ],
         compiler_params=pltpu.CompilerParams(vmem_limit_bytes=48 * 1024 * 1024),
-    )(x, coupling, elem_mats.reshape(terms, slots, slots, elems), face_links.reshape(chunks, 1, DIGIT))
+    )(extended, *lower[1:], *upper[1:], coupling, elem_mats.reshape(terms, slots, slots, elems), face_links.reshape(chunks, 1, DIGIT))
     from_next = lax.ppermute(out[:, :HALO], "space", down)
     from_prev = lax.ppermute(out[:, HALO + faces :], "space", up)
     mid = out[:, HALO : HALO + faces]

time: 123 us -> 110 us (0.89)
  waiting for transfers between devices: 54 us -> 34 us
  starting transfers between devices: 12 us -> 31.7 us
  between operations: 13.6 us -> 0.19 us
  other arithmetic: 2.76 us -> 0.93 us
  Pallas kernels: 35.6 us -> 37.2 us
    all_gather x1 -> x0, waiting for transfers between devices: 44.8 us -> none  [body(): x = lax.all_gather(extended, 'mode')]
    ppermute x0 -> x6, waiting for transfers between devices: none -> 24.8 us  [the longest x3 22.1 us: body(): upper.append(lax.ppermute(upper[-1], 'mode', left))]
    ppermute x0 -> x6, starting transfers between devices: none -> 17.2 us  [the longest x3 13.3 us: body(): lower.append(lax.ppermute(lower[-1], 'mode', right))]
    ppermute x1, starting transfers between devices: 3.66 us -> 6.18 us  [body(): from_prev = lax.ppermute(out[:, HALO + faces:], 'space', up)]
    unnamed x1 -> x0, other arithmetic: 1.82 us -> none
    pallas_call x1, Pallas kernels: 35.6 us -> 37.2 us  [body(): pl.pallas_call(functools.partial(kernel, dims), out_shape=jax.ShapeDtypeS...]
  transfers between devices with their start and end apart: 5 -> 10, of which waited for: 4 -> 9; matrix products, arithmetic and copies ran while one was open for 2% -> 2% of each run, Pallas kernels for 0% -> 0%
where the time goes in v1:
time: 110 us; the launch traced here: 108 us
  Pallas kernels  37.2 us (34%)
  waiting for transfers between devices  34 us (31%)
  starting transfers between devices  31.7 us (29%)
  local copies, waits for them, and re-layouts  3.64 us (3%)
    pallas_call x1, Pallas kernels, body(): pl.pallas_call(functools.partial(kernel, dims), out_shape=jax.ShapeDtypeS...  37.2 us
    ppermute x3, waiting for transfers between devices, body(): upper.append(lax.ppermute(upper[-1], 'mode', left))  22.1 us
    ppermute x3, starting transfers between devices, body(): lower.append(lax.ppermute(lower[-1], 'mode', right))  13.3 us
    ppermute x1, starting transfers between devices, body(): from_prev = lax.ppermute(out[:, HALO + faces:], 'space', up)  6.18 us
    ppermute x1, starting transfers between devices, body(): before = lax.ppermute(traces[:, faces - HALO:], 'space', up)  4.51 us
    ppermute x1, waiting for transfers between devices, body(): from_next = lax.ppermute(out[:, :HALO], 'space', down)  4.25 us
    ppermute x3, starting transfers between devices, body(): upper.append(lax.ppermute(upper[-1], 'mode', left))  3.85 us
    ppermute x1, waiting for transfers between devices, body(): after = lax.ppermute(traces[:, :HALO], 'space', down)  3.57 us
  transfers between devices with their start and end apart: 10, of which 9 were waited for; matrix products, arithmetic and copies ran while one was open for 2% of the time, Pallas kernels for 0%

profile of v1, /device:TPU:1, one launch (start us, length us, event | category | flops | bytes accessed | tf_op | source)
XLA Modules:
  0.0 108.5 jit_solution(968500527012694853)
XLA Ops:
  0.0 0.9 fusion.12
  0.9 4.5 %collective-permute-start = (f32[30,512]{1,0:T(8,128)S(1)}, f32[30,512]{1,0:T(8,128)S(1)}, u32[]{:S(2)}, u32[]{:S(2)}) collective-permute-start(f32[30,512]{1,0:T(8,128)S(1)} %get-tuple-element.11), channel_id=1, source_target_pairs={{0,1},{1,2},{2,3},{3,4},{4,5},{5,6},{6,7},{8,9},{9,10},{10,11},{11... | collective-permute-start | bytes 184328 | tf_op jit(solution)/shard_map/ppermute | solution.py:125
  5.5 1.9 %collective-permute-start.1 = (f32[30,512]{1,0:T(8,128)S(1)}, f32[30,512]{1,0:T(8,128)S(1)}, u32[]{:S(2)}, u32[]{:S(2)}) collective-permute-start(f32[30,512]{1,0:T(8,128)S(1)} %get-tuple-element.10), channel_id=1, source_target_pairs={{1,0},{2,1},{3,2},{4,3},{5,4},{6,5},{7,6},{9,8},{10,9},{11,10},{12... | collective-permute-start | bytes 184328 | tf_op jit(solution)/shard_map/ppermute | solution.py:126
  7.5 3.6 %collective-permute-done.1 = f32[30,512]{1,0:T(8,128)S(1)} collective-permute-done((f32[30,512]{1,0:T(8,128)S(1)}, f32[30,512]{1,0:T(8,128)S(1)}, u32[]{:S(2)}, u32[]{:S(2)}) %collective-permute-start.1) | collective-permute-done | bytes 61472 | tf_op jit(solution)/shard_map/ppermute | solution.py:126
  11.1 1.3 %collective-permute-start.5 = (f32[30,4096]{1,0:T(8,128)S(1)}, f32[30,4096]{1,0:T(8,128)S(1)}, u32[]{:S(2)}, u32[]{:S(2)}) collective-permute-start(f32[30,4096]{1,0:T(8,128)S(1)} %constant_dynamic-update-slice_fusion.own_ref), channel_id=1, source_target_pairs={{8,0},{16,8},{24,16},{9,1},{17,9},{25,17},{10,2},{18,10},{26,18},{... | collective-permute-start | bytes 1474568 | tf_op jit(solution)/shard_map/ppermute | solution.py:133
  12.4 4.0 %collective-permute-start.2 = (f32[30,4096]{1,0:T(8,128)S(1)}, f32[30,4096]{1,0:T(8,128)S(1)}, u32[]{:S(2)}, u32[]{:S(2)}) collective-permute-start(f32[30,4096]{1,0:T(8,128)S(1)} %constant_dynamic-update-slice_fusion.own_ref), channel_id=1, source_target_pairs={{0,8},{8,16},{16,24},{1,9},{9,17},{17,25},{2,10},{10,18},{18,26},{... | collective-permute-start | bytes 1474568 | tf_op jit(solution)/shard_map/ppermute | solution.py:132
  16.4 8.3 %collective-permute-done.5.refs_3_ = f32[30,4096]{1,0:T(8,128)S(1)} collective-permute-done((f32[30,4096]{1,0:T(8,128)S(1)}, f32[30,4096]{1,0:T(8,128)S(1)}, u32[]{:S(2)}, u32[]{:S(2)}) %collective-permute-start.5) | collective-permute-done | bytes 491552 | tf_op jit(solution)/shard_map/ppermute | solution.py:133
  24.6 1.3 %collective-permute-start.6 = (f32[30,4096]{1,0:T(8,128)S(1)}, f32[30,4096]{1,0:T(8,128)S(1)}, u32[]{:S(2)}, u32[]{:S(2)}) collective-permute-start(f32[30,4096]{1,0:T(8,128)S(1)} %collective-permute-done.5.refs_3_), channel_id=1, source_target_pairs={{8,0},{16,8},{24,16},{9,1},{17,9},{25,17},{10,2},{18,10},{26,18},{... | collective-permute-start | bytes 1474568 | tf_op jit(solution)/shard_map/ppermute | solution.py:133
  26.4 4.6 %collective-permute-start.3 = (f32[30,4096]{1,0:T(8,128)S(1)}, f32[30,4096]{1,0:T(8,128)}, u32[]{:S(2)}, u32[]{:S(2)}) collective-permute-start(f32[30,4096]{1,0:T(8,128)S(1)} %collective-permute-done.2.refs_0_), channel_id=1, source_target_pairs={{0,8},{8,16},{16,24},{1,9},{9,17},{17,25},{2,10},{10,18},{18,26},{... | collective-permute-start | bytes 1474568 | tf_op jit(solution)/shard_map/ppermute | solution.py:132
  31.1 8.2 %collective-permute-done.6.refs_4_ = f32[30,4096]{1,0:T(8,128)S(1)} collective-permute-done((f32[30,4096]{1,0:T(8,128)S(1)}, f32[30,4096]{1,0:T(8,128)S(1)}, u32[]{:S(2)}, u32[]{:S(2)}) %collective-permute-start.6) | collective-permute-done | bytes 491552 | tf_op jit(solution)/shard_map/ppermute | solution.py:133
  39.3 1.3 %collective-permute-start.7 = (f32[30,4096]{1,0:T(8,128)S(1)}, f32[30,4096]{1,0:T(8,128)}, u32[]{:S(2)}, u32[]{:S(2)}) collective-permute-start(f32[30,4096]{1,0:T(8,128)S(1)} %collective-permute-done.6.refs_4_), channel_id=1, source_target_pairs={{8,0},{16,8},{24,16},{9,1},{17,9},{25,17},{10,2},{18,10},{26,18},{... | collective-permute-start | bytes 1474568 | tf_op jit(solution)/shard_map/ppermute | solution.py:133
  40.6 0.8 collective-permute-done.3.refs_1_
  41.3 4.7 %collective-permute-start.4 = (f32[30,4096]{1,0:T(8,128)}, f32[30,4096]{1,0:T(8,128)}, u32[]{:S(2)}, u32[]{:S(2)}) collective-permute-start(f32[30,4096]{1,0:T(8,128)} %collective-permute-done.3.refs_1_), channel_id=1, source_target_pairs={{0,8},{8,16},{16,24},{1,9},{9,17},{17,25},{2,10},{10,18},{18,26},{... | collective-permute-start | bytes 1474568 | tf_op jit(solution)/shard_map/ppermute | solution.py:132
  46.1 1.2 %reshape.57.refs_7_ = f32[5,6,6,1024]{3,2,1,0:T(8,128)S(1)} reshape(f32[5,36,1024]{2,1,0:T(8,128)} %param.7) | data formatting | bytes 1474560 | tf_op jit(solution)/shard_map/reshape | solution.py:151
  48.0 0.7 copy-done.4
  48.7 0.8 convolution_add_fusion.refs_6_
  49.5 5.7 %collective-permute-done.7.refs_5_ = f32[30,4096]{1,0:T(8,128)} collective-permute-done((f32[30,4096]{1,0:T(8,128)S(1)}, f32[30,4096]{1,0:T(8,128)}, u32[]{:S(2)}, u32[]{:S(2)}) %collective-permute-start.7) | collective-permute-done | bytes 491552 | tf_op jit(solution)/shard_map/ppermute | solution.py:133
  55.2 1.5 %collective-permute-done.4.refs_2_ = f32[30,4096]{1,0:T(8,128)} collective-permute-done((f32[30,4096]{1,0:T(8,128)}, f32[30,4096]{1,0:T(8,128)}, u32[]{:S(2)}, u32[]{:S(2)}) %collective-permute-start.4) | collective-permute-done | bytes 491552 | tf_op jit(solution)/shard_map/ppermute | solution.py:132
  56.7 37.2 %shard_map.64 = f32[30,4096]{1,0:T(8,128)S(1)} custom-call(f32[30,4096]{1,0:T(8,128)S(1)} %constant_dynamic-update-slice_fusion.own_ref, f32[30,4096]{1,0:T(8,128)S(1)} %collective-permute-done.2.refs_0_, f32[30,4096]{1,0:T(8,128)} %collective-permute-done.3.refs_1_, f32[30,4096]{1,0:T(8,128)} %collective-permute-done.4.refs_2_, ...), custom_call_target="tpu_custom_call" | custom-call | tf_op jit(solution)/shard_map/pallas_call | solution.py:138
  93.9 6.2 %collective-permute-start.8 = (f32[30,512]{1,0:T(8,128)S(1)}, f32[30,512]{1,0:T(8,128)S(1)}, u32[]{:S(2)}, u32[]{:S(2)}) collective-permute-start(f32[30,512]{1,0:T(8,128)S(1)} %slice.44), channel_id=1, source_target_pairs={{0,1},{1,2},{2,3},{3,4},{4,5},{5,6},{6,7},{8,9},{9,10},{10,11},{11... | collective-permute-start | bytes 184328 | tf_op jit(solution)/shard_map/ppermute | solution.py:153
  100.1 1.3 %collective-permute-done.8 = f32[30,512]{1,0:T(8,128)S(1)} collective-permute-done((f32[30,512]{1,0:T(8,128)S(1)}, f32[30,512]{1,0:T(8,128)S(1)}, u32[]{:S(2)}, u32[]{:S(2)}) %collective-permute-start.8) | collective-permute-done | bytes 61472 | tf_op jit(solution)/shard_map/ppermute | solution.py:153
  101.5 1.9 %collective-permute-start.9 = (f32[30,512]{1,0:T(8,128)S(1)}, f32[30,512]{1,0:T(8,128)S(1)}, u32[]{:S(2)}, u32[]{:S(2)}) collective-permute-start(f32[30,512]{1,0:T(8,128)S(1)} %get-tuple-element.9), channel_id=1, source_target_pairs={{1,0},{2,1},{3,2},{4,3},{5,4},{6,5},{7,6},{9,8},{10,9},{11,10},{12... | collective-permute-start | bytes 184328 | tf_op jit(solution)/shard_map/ppermute | solution.py:152
  103.4 4.3 %collective-permute-done.9 = f32[30,512]{1,0:T(8,128)S(1)} collective-permute-done((f32[30,512]{1,0:T(8,128)S(1)}, f32[30,512]{1,0:T(8,128)S(1)}, u32[]{:S(2)}, u32[]{:S(2)}) %collective-permute-start.9) | collective-permute-done | bytes 61472 | tf_op jit(solution)/shard_map/ppermute | solution.py:152
  107.7 0.8 pad_maximum_fusion
  (23 shorter events, 1.4 us)
Async XLA Ops:
  0.0 7.4 %copy-start = (f32[30,3072]{1,0:T(8,128)S(1)}, f32[30,3072]{1,0:T(8,128)}, u32[]{:S(2)}) copy-start(f32[30,3072]{1,0:T(8,128)} %param.6) | copy-start | bytes 1105924
  0.9 6.4 %collective-permute-start = (f32[30,512]{1,0:T(8,128)S(1)}, f32[30,512]{1,0:T(8,128)S(1)}, u32[]{:S(2)}, u32[]{:S(2)}) collective-permute-start(f32[30,512]{1,0:T(8,128)S(1)} %get-tuple-element.11), channel_id=1, source_target_pairs={{0,1},{1,2},{2,3},{3,4},{4,5},{5,6},{6,7},{8,9},{9,10},{10,11},{11... | collective-permute-start | bytes 184328 | tf_op jit(solution)/shard_map/ppermute | solution.py:125
  5.5 5.6 %collective-permute-start.1 = (f32[30,512]{1,0:T(8,128)S(1)}, f32[30,512]{1,0:T(8,128)S(1)}, u32[]{:S(2)}, u32[]{:S(2)}) collective-permute-start(f32[30,512]{1,0:T(8,128)S(1)} %get-tuple-element.10), channel_id=1, source_target_pairs={{1,0},{2,1},{3,2},{4,3},{5,4},{6,5},{7,6},{9,8},{10,9},{11,10},{12... | collective-permute-start | bytes 184328 | tf_op jit(solution)/shard_map/ppermute | solution.py:126
  7.5 23.5 %copy-start.2 = (s32[2,1440]{1,0:T(2,128)S(1)}, s32[2,1440]{1,0:T(2,128)}, u32[]{:S(2)}) copy-start(s32[2,1440]{1,0:T(2,128)} %param.9) | copy-start | bytes 34564
  11.0 35.0 %copy-start.1 = (s32[6,1024]{1,0:T(8,128)S(1)}, s32[6,1024]{1,0:T(8,128)}, u32[]{:S(2)}) copy-start(s32[6,1024]{1,0:T(8,128)} %param.8) | copy-start | bytes 73732
  11.1 13.6 %collective-permute-start.5 = (f32[30,4096]{1,0:T(8,128)S(1)}, f32[30,4096]{1,0:T(8,128)S(1)}, u32[]{:S(2)}, u32[]{:S(2)}) collective-permute-start(f32[30,4096]{1,0:T(8,128)S(1)} %constant_dynamic-update-slice_fusion.own_ref), channel_id=1, source_target_pairs={{8,0},{16,8},{24,16},{9,1},{17,9},{25,17},{10,2},{18,10},{26,18},{... | collective-permute-start | bytes 1474568 | tf_op jit(solution)/shard_map/ppermute | solution.py:133
  12.4 14.0 %collective-permute-start.2 = (f32[30,4096]{1,0:T(8,128)S(1)}, f32[30,4096]{1,0:T(8,128)S(1)}, u32[]{:S(2)}, u32[]{:S(2)}) collective-permute-start(f32[30,4096]{1,0:T(8,128)S(1)} %constant_dynamic-update-slice_fusion.own_ref), channel_id=1, source_target_pairs={{0,8},{8,16},{16,24},{1,9},{9,17},{17,25},{2,10},{10,18},{18,26},{... | collective-permute-start | bytes 1474568 | tf_op jit(solution)/shard_map/ppermute | solution.py:132
  24.6 14.6 %collective-permute-start.6 = (f32[30,4096]{1,0:T(8,128)S(1)}, f32[30,4096]{1,0:T(8,128)S(1)}, u32[]{:S(2)}, u32[]{:S(2)}) collective-permute-start(f32[30,4096]{1,0:T(8,128)S(1)} %collective-permute-done.5.refs_3_), channel_id=1, source_target_pairs={{8,0},{16,8},{24,16},{9,1},{17,9},{25,17},{10,2},{18,10},{26,18},{... | collective-permute-start | bytes 1474568 | tf_op jit(solution)/shard_map/ppermute | solution.py:133
  26.4 14.9 %collective-permute-start.3 = (f32[30,4096]{1,0:T(8,128)S(1)}, f32[30,4096]{1,0:T(8,128)}, u32[]{:S(2)}, u32[]{:S(2)}) collective-permute-start(f32[30,4096]{1,0:T(8,128)S(1)} %collective-permute-done.2.refs_0_), channel_id=1, source_target_pairs={{0,8},{8,16},{16,24},{1,9},{9,17},{17,25},{2,10},{10,18},{18,26},{... | collective-permute-start | bytes 1474568 | tf_op jit(solution)/shard_map/ppermute | solution.py:132
  39.3 15.9 %collective-permute-start.7 = (f32[30,4096]{1,0:T(8,128)S(1)}, f32[30,4096]{1,0:T(8,128)}, u32[]{:S(2)}, u32[]{:S(2)}) collective-permute-start(f32[30,4096]{1,0:T(8,128)S(1)} %collective-permute-done.6.refs_4_), channel_id=1, source_target_pairs={{8,0},{16,8},{24,16},{9,1},{17,9},{25,17},{10,2},{18,10},{26,18},{... | collective-permute-start | bytes 1474568 | tf_op jit(solution)/shard_map/ppermute | solution.py:133
  41.3 15.4 %collective-permute-start.4 = (f32[30,4096]{1,0:T(8,128)}, f32[30,4096]{1,0:T(8,128)}, u32[]{:S(2)}, u32[]{:S(2)}) collective-permute-start(f32[30,4096]{1,0:T(8,128)} %collective-permute-done.3.refs_1_), channel_id=1, source_target_pairs={{0,8},{8,16},{16,24},{1,9},{9,17},{17,25},{2,10},{10,18},{18,26},{... | collective-permute-start | bytes 1474568 | tf_op jit(solution)/shard_map/ppermute | solution.py:132
  47.3 0.7 copy-start.3
  48.0 0.7 copy-start.4
  93.9 7.5 %collective-permute-start.8 = (f32[30,512]{1,0:T(8,128)S(1)}, f32[30,512]{1,0:T(8,128)S(1)}, u32[]{:S(2)}, u32[]{:S(2)}) collective-permute-start(f32[30,512]{1,0:T(8,128)S(1)} %slice.44), channel_id=1, source_target_pairs={{0,1},{1,2},{2,3},{3,4},{4,5},{5,6},{6,7},{8,9},{9,10},{10,11},{11... | collective-permute-start | bytes 184328 | tf_op jit(solution)/shard_map/ppermute | solution.py:153
  101.5 6.2 %collective-permute-start.9 = (f32[30,512]{1,0:T(8,128)S(1)}, f32[30,512]{1,0:T(8,128)S(1)}, u32[]{:S(2)}, u32[]{:S(2)}) collective-permute-start(f32[30,512]{1,0:T(8,128)S(1)} %get-tuple-element.9), channel_id=1, source_target_pairs={{1,0},{2,1},{3,2},{4,3},{5,4},{6,5},{7,6},{9,8},{10,9},{11,10},{12... | collective-permute-start | bytes 184328 | tf_op jit(solution)/shard_map/ppermute | solution.py:152

commit v2 on v1

--- a/solution.py
+++ b/solution.py
@@ -34,42 +34,74 @@
     return high, (value - high.astype(jnp.float32)).astype(BF)
 
 
-def kernel(dims, own_ref, *refs):
-    groups = dims[0]
-    lower, upper = refs[: groups - 1], refs[groups - 1 : 2 * groups - 2]
-    compute(dims, own_ref, lower, upper, *refs[2 * groups - 2 :])
-
-
-def compute(dims, own_ref, lower, upper, coupling_ref, mats_ref, links_ref, out_ref, low_ref, x2_ref, z_ref, v_ref, acc_ref):
+def digit_table(links):
+    ids = lax.broadcasted_iota(jnp.int32, (DIGIT, DIGIT), 0)
+    return (ids == links % DIGIT).astype(jnp.float32).astype(BF)
+
+
+def gather_kernel(dims, *refs):
     groups, rows, pad, terms, slots, elems, ext = dims
+    *shards, links_ref, g_ref, x2_ref = refs
     tops = ext // DIGIT
-    per_slot = elems // DIGIT
-    chunks = slots * per_slot
-    modes = groups * pad
+    modes = len(shards) * pad
     x2_ref[...] = jnp.zeros_like(x2_ref)
-    for d in range(groups):
+    for d, shard in enumerate(shards):
         for h in range(tops):
-            at = slice(h * DIGIT, (h + 1) * DIGIT)
-            block = own_ref[:, at] if d == 0 else upper[d - 1][:, at] + lower[groups - d - 1][:, at]
-            high, low = split(block)
+            high, low = split(shard[:, h * DIGIT : (h + 1) * DIGIT])
             base = h * modes + d * pad
             x2_ref[0, base : base + rows, :] = high
             x2_ref[1, base : base + rows, :] = low
-    c_high, c_low = split(coupling_ref[...])
-
-    @pl.loop(0, chunks)
+
+    @pl.loop(0, slots * elems // DIGIT)
     def _(c):
         links = links_ref[c]
-        ids = lax.broadcasted_iota(jnp.int32, (DIGIT, DIGIT), 0)
-        table = (ids == links % DIGIT).astype(jnp.float32).astype(BF)
-        low_ref[c] = table
+        table = digit_table(links)
         found = jnp.dot(x2_ref[0], table, preferred_element_type=jnp.float32)
         found = found + jnp.dot(x2_ref[1], table, preferred_element_type=jnp.float32)
         tops_of = links // DIGIT
         g = jnp.zeros((modes, DIGIT), jnp.float32)
         for h in range(tops):
             g = jnp.where(tops_of == h, found[h * modes : (h + 1) * modes], g)
-        g_high, g_low = split(g)
+        g_ref[c] = g
+
+
+def gather(dims, shards, links):
+    groups, rows, pad, terms, slots, elems, ext = dims
+    chunks, modes, tops = links.shape[0], len(shards) * pad, ext // DIGIT
+    vmem = pl.BlockSpec(memory_space=pltpu.VMEM)
+    return pl.pallas_call(
+        functools.partial(gather_kernel, dims),
+        out_shape=jax.ShapeDtypeStruct((chunks, modes, DIGIT), jnp.float32),
+        in_specs=[vmem] * (len(shards) + 1),
+        out_specs=vmem,
+        scratch_shapes=[pltpu.VMEM((2, tops * modes, DIGIT), BF)],
+        cost_estimate=pl.CostEstimate(
+            flops=16 * tops * modes * DIGIT * chunks * DIGIT,
+            bytes_accessed=4 * modes * (ext + chunks * DIGIT),
+            transcendentals=0,
+        ),
+        compiler_params=pltpu.CompilerParams(vmem_limit_bytes=24 * 1024 * 1024),
+    )(*shards, links)
+
+
+def kernel(dims, *refs):
+    groups = dims[0]
+    compute(dims, refs[0], refs[1:groups], *refs[groups:])
+
+
+def compute(dims, own_ref, step_refs, coupling_ref, mats_ref, links_ref, out_ref, z_ref, v_ref, acc_ref):
+    groups, rows, pad, terms, slots, elems, ext = dims
+    tops = ext // DIGIT
+    per_slot = elems // DIGIT
+    chunks = slots * per_slot
+    c_high, c_low = split(coupling_ref[...])
+
+    @pl.loop(0, chunks)
+    def _(c):
+        blocks = [own_ref[c]] + [
+            step_refs[d - 1][c, pad:, :] + step_refs[groups - d - 1][c, :pad, :] for d in range(1, groups)
+        ]
+        g_high, g_low = split(jnp.concatenate(blocks, axis=0))
         z = jnp.dot(c_high, g_high, preferred_element_type=jnp.float32)
         z = z + jnp.dot(c_high, g_low, preferred_element_type=jnp.float32)
         z_ref[c] = z + jnp.dot(c_low, g_high, preferred_element_type=jnp.float32)
@@ -98,7 +130,7 @@
         parts = [v * (tops_of == h).astype(jnp.float32).astype(BF) for h in range(tops)]
         acc_ref[...] += lax.dot_general(
             jnp.concatenate(parts, axis=0),
-            low_ref[c],
+            digit_table(links_ref[c]),
             (((1,), (1,)), ((), ())),
             preferred_element_type=jnp.float32,
         )
@@ -134,21 +166,22 @@
     dims = (groups, rows, pad, terms, slots, elems, ext)
     tops = ext // DIGIT
     chunks = slots * elems // DIGIT
+    links = face_links.reshape(chunks, 1, DIGIT)
+    own = gather(dims, [extended], links)
+    steps = [gather(dims, [lower[r], upper[r]], links) for r in range(1, groups)]
     vmem = pl.BlockSpec(memory_space=pltpu.VMEM)
     out = pl.pallas_call(
         functools.partial(kernel, dims),
         out_shape=jax.ShapeDtypeStruct((rows, ext), jnp.float32),
-        in_specs=[vmem] * (2 * groups + 2),
+        in_specs=[vmem] * (groups + 3),
         out_specs=vmem,
         scratch_shapes=[
-            pltpu.VMEM((chunks, DIGIT, DIGIT), BF),
-            pltpu.VMEM((2, tops * groups * pad, DIGIT), BF),
             pltpu.VMEM((chunks, terms * pad, DIGIT), jnp.float32),
             pltpu.VMEM((chunks, 2 * pad, DIGIT), BF),
             pltpu.VMEM((2 * pad * tops, DIGIT), jnp.float32),
         ],
         compiler_params=pltpu.CompilerParams(vmem_limit_bytes=48 * 1024 * 1024),
-    )(extended, *lower[1:], *upper[1:], coupling, elem_mats.reshape(terms, slots, slots, elems), face_links.reshape(chunks, 1, DIGIT))
+    )(own, *steps, coupling, elem_mats.reshape(terms, slots, slots, elems), links)
     from_next = lax.ppermute(out[:, :HALO], "space", down)
     from_prev = lax.ppermute(out[:, HALO + faces :], "space", up)
     mid = out[:, HALO : HALO + faces]

time: 110 us -> 104 us (0.945)
  waiting for transfers between devices: 34 us -> 10.3 us
  Pallas kernels: 37.2 us -> 57.4 us
  starting transfers between devices: 31.7 us -> 28.5 us
  other arithmetic: 0.93 us -> 3.12 us
  local copies, waits for them, and re-layouts: 3.64 us -> 2.32 us
    pallas_call x0 -> x4, Pallas kernels: none -> 40 us  [gather(): pl.pallas_call(functools.partial(gather_kernel, dims), out_shape=jax.Shap...]
    pallas_call x1, Pallas kernels: 37.2 us -> 17.3 us  [body(): pl.pallas_call(functools.partial(kernel, dims), out_shape=jax.ShapeDtypeS...]
    ppermute x3, waiting for transfers between devices: 22.1 us -> 3.22 us  [body(): upper.append(lax.ppermute(upper[-1], 'mode', left))]
    ppermute x1, waiting for transfers between devices: 3.57 us -> 0.01 us  [body(): after = lax.ppermute(traces[:, :HALO], 'space', down)]
    ppermute x3, starting transfers between devices: 13.3 us -> 11.4 us  [body(): lower.append(lax.ppermute(lower[-1], 'mode', right))]
    ppermute x1, starting transfers between devices: 6.18 us -> 4.9 us  [body(): from_prev = lax.ppermute(out[:, HALO + faces:], 'space', up)]
    ppermute x3, waiting for transfers between devices: 2.71 us -> 1.5 us  [body(): lower.append(lax.ppermute(lower[-1], 'mode', right))]
    reshape x1, local copies, waits for them, and re-layouts: 1.24 us -> 0.1 us  [body(): elem_mats.reshape(terms, slots, slots, elems)]
  transfers between devices with their start and end apart: 10 -> 10, of which waited for: 9 -> 4; matrix products, arithmetic and copies ran while one was open for 2% -> 4% of each run, Pallas kernels for 0% -> 28%
where the time goes in v2:
time: 104 us; the launch traced here: 103 us
  Pallas kernels  57.4 us (55%)
  starting transfers between devices  28.5 us (27%)
  waiting for transfers between devices  10.3 us (10%)
  other arithmetic  3.12 us (3%)
  local copies, waits for them, and re-layouts  2.32 us (2%)
  matrix products  1.56 us (2%)
    pallas_call x4, Pallas kernels, gather(): pl.pallas_call(functools.partial(gather_kernel, dims), out_shape=jax.Shap...  40 us
    pallas_call x1, Pallas kernels, body(): pl.pallas_call(functools.partial(kernel, dims), out_shape=jax.ShapeDtypeS...  17.3 us
    ppermute x3, starting transfers between devices, body(): lower.append(lax.ppermute(lower[-1], 'mode', right))  11.4 us
    ppermute x1, starting transfers between devices, body(): from_prev = lax.ppermute(out[:, HALO + faces:], 'space', up)  4.9 us
    ppermute x1, starting transfers between devices, body(): before = lax.ppermute(traces[:, faces - HALO:], 'space', up)  4.51 us
    ppermute x1, waiting for transfers between devices, body(): from_next = lax.ppermute(out[:, :HALO], 'space', down)  4.25 us
    ppermute x3, starting transfers between devices, body(): upper.append(lax.ppermute(upper[-1], 'mode', left))  3.88 us
    ppermute x3, waiting for transfers between devices, body(): upper.append(lax.ppermute(upper[-1], 'mode', left))  3.22 us
  transfers between devices with their start and end apart: 10, of which 4 were waited for; matrix products, arithmetic and copies ran while one was open for 4% of the time, Pallas kernels for 28%

profile of v2, /device:TPU:1, one launch (start us, length us, event | category | flops | bytes accessed | tf_op | source)
XLA Modules:
  0.0 103.5 jit_solution(11399027919086119145)
XLA Ops:
  0.0 1.0 fusion.12
  1.0 4.5 %collective-permute-start = (f32[30,512]{1,0:T(8,128)S(1)}, f32[30,512]{1,0:T(8,128)S(1)}, u32[]{:S(2)}, u32[]{:S(2)}) collective-permute-start(f32[30,512]{1,0:T(8,128)S(1)} %get-tuple-element.11), channel_id=1, source_target_pairs={{0,1},{1,2},{2,3},{3,4},{4,5},{5,6},{6,7},{8,9},{9,10},{10,11},{11... | collective-permute-start | bytes 184328 | tf_op jit(solution)/shard_map/ppermute | solution.py:157
  5.5 1.9 %collective-permute-start.1 = (f32[30,512]{1,0:T(8,128)S(1)}, f32[30,512]{1,0:T(8,128)S(1)}, u32[]{:S(2)}, u32[]{:S(2)}) collective-permute-start(f32[30,512]{1,0:T(8,128)S(1)} %get-tuple-element.10), channel_id=1, source_target_pairs={{1,0},{2,1},{3,2},{4,3},{5,4},{6,5},{7,6},{9,8},{10,9},{11,10},{12... | collective-permute-start | bytes 184328 | tf_op jit(solution)/shard_map/ppermute | solution.py:158
  7.4 0.9 divide_reduce_fusion
  9.8 1.6 %convolution_add_fusion.refs_4_ = f32[160,128]{1,0:T(8,128)S(1)} fusion(f32[1440]{0:T(1024)} %param.11, s32[1440]{0:T(1024)S(1)} %get-tuple-element.13, s32[1440]{0:T(1024)S(1)} %get-tuple-element.12, pred[160]{0:T(512)(128)(4,1)S(1)} %iota_compare_fusion.5), kind=kOutput, calls=%fused_computation | convolution fusion | flops 354621440 | bytes 99360 | tf_op jit(solution)/shard_map/dot_general | solution.py:27
  11.6 3.2 %collective-permute-start.2 = (f32[30,4096]{1,0:T(8,128)S(1)}, f32[30,4096]{1,0:T(8,128)S(1)}, u32[]{:S(2)}, u32[]{:S(2)}) collective-permute-start(f32[30,4096]{1,0:T(8,128)S(1)} %constant_dynamic-update-slice_fusion.refs_0_), channel_id=1, source_target_pairs={{0,8},{8,16},{16,24},{1,9},{9,17},{17,25},{2,10},{10,18},{18,26},{... | collective-permute-start | bytes 1474568 | tf_op jit(solution)/shard_map/ppermute | solution.py:164
  14.9 1.3 %collective-permute-start.3 = (f32[30,4096]{1,0:T(8,128)S(1)}, f32[30,4096]{1,0:T(8,128)S(1)}, u32[]{:S(2)}, u32[]{:S(2)}) collective-permute-start(f32[30,4096]{1,0:T(8,128)S(1)} %constant_dynamic-update-slice_fusion.refs_0_), channel_id=1, source_target_pairs={{8,0},{16,8},{24,16},{9,1},{17,9},{25,17},{10,2},{18,10},{26,18},{... | collective-permute-start | bytes 1474568 | tf_op jit(solution)/shard_map/ppermute | solution.py:165
  16.2 7.5 %shard_map.64.refs_0_ = f32[24,32,256]{2,1,0:T(8,128)S(1)} custom-call(f32[30,4096]{1,0:T(8,128)S(1)} %constant_dynamic-update-slice_fusion.refs_0_, s32[24,1,256]{2,1,0:T(1,128)S(1)} %reshape.57.refs_1_.refs_2_.refs_6_), custom_call_target="tpu_custom_call" | custom-call | flops 12884901888 | bytes 1310720 | tf_op jit(solution)/shard_map/pallas_call | solution.py:72
  23.6 1.5 %collective-permute-done.2.refs_0_ = f32[30,4096]{1,0:T(8,128)S(1)} collective-permute-done((f32[30,4096]{1,0:T(8,128)S(1)}, f32[30,4096]{1,0:T(8,128)S(1)}, u32[]{:S(2)}, u32[]{:S(2)}) %collective-permute-start.2) | collective-permute-done | bytes 491552 | tf_op jit(solution)/shard_map/ppermute | solution.py:164
  25.1 4.1 %collective-permute-start.4 = (f32[30,4096]{1,0:T(8,128)S(1)}, f32[30,4096]{1,0:T(8,128)S(1)}, u32[]{:S(2)}, u32[]{:S(2)}) collective-permute-start(f32[30,4096]{1,0:T(8,128)S(1)} %collective-permute-done.2.refs_0_), channel_id=1, source_target_pairs={{0,8},{8,16},{16,24},{1,9},{9,17},{17,25},{2,10},{10,18},{18,26},{... | collective-permute-start | bytes 1474568 | tf_op jit(solution)/shard_map/ppermute | solution.py:164
  29.3 1.3 %collective-permute-start.5 = (f32[30,4096]{1,0:T(8,128)S(1)}, f32[30,4096]{1,0:T(8,128)S(1)}, u32[]{:S(2)}, u32[]{:S(2)}) collective-permute-start(f32[30,4096]{1,0:T(8,128)S(1)} %collective-permute-done.3.refs_1_), channel_id=1, source_target_pairs={{8,0},{16,8},{24,16},{9,1},{17,9},{25,17},{10,2},{18,10},{26,18},{... | collective-permute-start | bytes 1474568 | tf_op jit(solution)/shard_map/ppermute | solution.py:165
  30.6 10.9 %shard_map.65.refs_1_ = f32[24,64,256]{2,1,0:T(8,128)S(1)} custom-call(f32[30,4096]{1,0:T(8,128)S(1)} %collective-permute-done.2.refs_0_, f32[30,4096]{1,0:T(8,128)S(1)} %collective-permute-done.3.refs_1_, s32[24,1,256]{2,1,0:T(1,128)S(1)} %reshape.57.refs_1_.refs_2_.refs_6_), custom_call_target="tpu_custom_call" | custom-call | flops 25769803776 | bytes 2621440 | tf_op jit(solution)/shard_map/pallas_call | solution.py:72
  41.4 4.0 %collective-permute-start.6 = (f32[30,4096]{1,0:T(8,128)S(1)}, f32[30,4096]{1,0:T(8,128)S(1)}, u32[]{:S(2)}, u32[]{:S(2)}) collective-permute-start(f32[30,4096]{1,0:T(8,128)S(1)} %collective-permute-done.4.refs_0_), channel_id=1, source_target_pairs={{0,8},{8,16},{16,24},{1,9},{9,17},{17,25},{2,10},{10,18},{18,26},{... | collective-permute-start | bytes 1474568 | tf_op jit(solution)/shard_map/ppermute | solution.py:164
  45.5 1.3 %collective-permute-start.7 = (f32[30,4096]{1,0:T(8,128)S(1)}, f32[30,4096]{1,0:T(8,128)S(1)}, u32[]{:S(2)}, u32[]{:S(2)}) collective-permute-start(f32[30,4096]{1,0:T(8,128)S(1)} %collective-permute-done.5.refs_1_), channel_id=1, source_target_pairs={{8,0},{16,8},{24,16},{9,1},{17,9},{25,17},{10,2},{18,10},{26,18},{... | collective-permute-start | bytes 1474568 | tf_op jit(solution)/shard_map/ppermute | solution.py:165
  46.8 10.9 %shard_map.66.refs_2_ = f32[24,64,256]{2,1,0:T(8,128)S(1)} custom-call(f32[30,4096]{1,0:T(8,128)S(1)} %collective-permute-done.4.refs_0_, f32[30,4096]{1,0:T(8,128)S(1)} %collective-permute-done.5.refs_1_, s32[24,1,256]{2,1,0:T(1,128)S(1)} %reshape.57.refs_1_.refs_2_.refs_6_), custom_call_target="tpu_custom_call" | custom-call | flops 25769803776 | bytes 2621440 | tf_op jit(solution)/shard_map/pallas_call | solution.py:72
  57.7 3.2 %collective-permute-done.7.refs_1_ = f32[30,4096]{1,0:T(8,128)S(1)} collective-permute-done((f32[30,4096]{1,0:T(8,128)S(1)}, f32[30,4096]{1,0:T(8,128)S(1)}, u32[]{:S(2)}, u32[]{:S(2)}) %collective-permute-start.7) | collective-permute-done | bytes 491552 | tf_op jit(solution)/shard_map/ppermute | solution.py:165
  60.9 10.9 %shard_map.67.refs_3_ = f32[24,64,256]{2,1,0:T(8,128)S(1)} custom-call(f32[30,4096]{1,0:T(8,128)S(1)} %collective-permute-done.6.refs_0_, f32[30,4096]{1,0:T(8,128)S(1)} %collective-permute-done.7.refs_1_, s32[24,1,256]{2,1,0:T(1,128)S(1)} %reshape.57.refs_1_.refs_2_.refs_6_), custom_call_target="tpu_custom_call" | custom-call | flops 25769803776 | bytes 2621440 | tf_op jit(solution)/shard_map/pallas_call | solution.py:72
  71.7 1.1 %copy-done = f32[24,64,256]{2,1,0:T(8,128)} copy-done((f32[24,64,256]{2,1,0:T(8,128)}, f32[24,64,256]{2,1,0:T(8,128)S(1)}, u32[]{:S(2)}) %copy-start) | copy-done | bytes 1572888
  72.9 17.3 %shard_map.68 = f32[30,4096]{1,0:T(8,128)S(1)} custom-call(f32[24,32,256]{2,1,0:T(8,128)S(1)} %shard_map.64.refs_0_, f32[24,64,256]{2,1,0:T(8,128)S(1)} %shard_map.65.refs_1_, f32[24,64,256]{2,1,0:T(8,128)S(1)} %shard_map.66.refs_2_, f32[24,64,256]{2,1,0:T(8,128)} %copy-done, f32[160,128]{1,0:T(8,128)S(1)} %convolution_add_fusion.refs_4_, ...), custom_call_target="tpu_custom_call" | custom-call | tf_op jit(solution)/shard_map/pallas_call | solution.py:173
  90.2 4.9 %collective-permute-start.8 = (f32[30,512]{1,0:T(8,128)S(1)}, f32[30,512]{1,0:T(8,128)S(1)}, u32[]{:S(2)}, u32[]{:S(2)}) collective-permute-start(f32[30,512]{1,0:T(8,128)S(1)} %slice.44), channel_id=1, source_target_pairs={{0,1},{1,2},{2,3},{3,4},{4,5},{5,6},{6,7},{8,9},{9,10},{10,11},{11... | collective-permute-start | bytes 184328 | tf_op jit(solution)/shard_map/ppermute | solution.py:186
  95.1 1.3 %collective-permute-done.8 = f32[30,512]{1,0:T(8,128)S(1)} collective-permute-done((f32[30,512]{1,0:T(8,128)S(1)}, f32[30,512]{1,0:T(8,128)S(1)}, u32[]{:S(2)}, u32[]{:S(2)}) %collective-permute-start.8) | collective-permute-done | bytes 61472 | tf_op jit(solution)/shard_map/ppermute | solution.py:186
  96.5 1.9 %collective-permute-start.9 = (f32[30,512]{1,0:T(8,128)S(1)}, f32[30,512]{1,0:T(8,128)S(1)}, u32[]{:S(2)}, u32[]{:S(2)}) collective-permute-start(f32[30,512]{1,0:T(8,128)S(1)} %get-tuple-element.9), channel_id=1, source_target_pairs={{1,0},{2,1},{3,2},{4,3},{5,4},{6,5},{7,6},{9,8},{10,9},{11,10},{12... | collective-permute-start | bytes 184328 | tf_op jit(solution)/shard_map/ppermute | solution.py:185
  98.4 4.3 %collective-permute-done.9 = f32[30,512]{1,0:T(8,128)S(1)} collective-permute-done((f32[30,512]{1,0:T(8,128)S(1)}, f32[30,512]{1,0:T(8,128)S(1)}, u32[]{:S(2)}, u32[]{:S(2)}) %collective-permute-start.9) | collective-permute-done | bytes 61472 | tf_op jit(solution)/shard_map/ppermute | solution.py:185
  102.7 0.8 pad_maximum_fusion
  (25 shorter events, 1.7 us)
Async XLA Ops:
  0.0 11.4 %copy-start.3 = (s32[6,1024]{1,0:T(8,128)S(1)}, s32[6,1024]{1,0:T(8,128)}, u32[]{:S(2)}) copy-start(s32[6,1024]{1,0:T(8,128)} %param.8) | copy-start | bytes 73732
  0.0 11.4 %copy-start.1 = (f32[5,36,1024]{2,1,0:T(8,128)S(1)}, f32[5,36,1024]{2,1,0:T(8,128)}, u32[]{:S(2)}) copy-start(f32[5,36,1024]{2,1,0:T(8,128)} %param.7) | copy-start | bytes 2211844
  1.0 10.6 %collective-permute-start = (f32[30,512]{1,0:T(8,128)S(1)}, f32[30,512]{1,0:T(8,128)S(1)}, u32[]{:S(2)}, u32[]{:S(2)}) collective-permute-start(f32[30,512]{1,0:T(8,128)S(1)} %get-tuple-element.11), channel_id=1, source_target_pairs={{0,1},{1,2},{2,3},{3,4},{4,5},{5,6},{6,7},{8,9},{9,10},{10,11},{11... | collective-permute-start | bytes 184328 | tf_op jit(solution)/shard_map/ppermute | solution.py:157
  5.5 6.1 %collective-permute-start.1 = (f32[30,512]{1,0:T(8,128)S(1)}, f32[30,512]{1,0:T(8,128)S(1)}, u32[]{:S(2)}, u32[]{:S(2)}) collective-permute-start(f32[30,512]{1,0:T(8,128)S(1)} %get-tuple-element.10), channel_id=1, source_target_pairs={{1,0},{2,1},{3,2},{4,3},{5,4},{6,5},{7,6},{9,8},{10,9},{11,10},{12... | collective-permute-start | bytes 184328 | tf_op jit(solution)/shard_map/ppermute | solution.py:158
  9.8 1.8 %copy-start.2 = (f32[30,3072]{1,0:T(8,128)S(1)}, f32[30,3072]{1,0:T(8,128)}, u32[]{:S(2)}) copy-start(f32[30,3072]{1,0:T(8,128)} %param.6) | copy-start | bytes 1105924
  11.6 13.5 %collective-permute-start.2 = (f32[30,4096]{1,0:T(8,128)S(1)}, f32[30,4096]{1,0:T(8,128)S(1)}, u32[]{:S(2)}, u32[]{:S(2)}) collective-permute-start(f32[30,4096]{1,0:T(8,128)S(1)} %constant_dynamic-update-slice_fusion.refs_0_), channel_id=1, source_target_pairs={{0,8},{8,16},{16,24},{1,9},{9,17},{17,25},{2,10},{10,18},{18,26},{... | collective-permute-start | bytes 1474568 | tf_op jit(solution)/shard_map/ppermute | solution.py:164
  14.9 14.4 %collective-permute-start.3 = (f32[30,4096]{1,0:T(8,128)S(1)}, f32[30,4096]{1,0:T(8,128)S(1)}, u32[]{:S(2)}, u32[]{:S(2)}) collective-permute-start(f32[30,4096]{1,0:T(8,128)S(1)} %constant_dynamic-update-slice_fusion.refs_0_), channel_id=1, source_target_pairs={{8,0},{16,8},{24,16},{9,1},{17,9},{25,17},{10,2},{18,10},{26,18},{... | collective-permute-start | bytes 1474568 | tf_op jit(solution)/shard_map/ppermute | solution.py:165
  25.1 16.3 %collective-permute-start.4 = (f32[30,4096]{1,0:T(8,128)S(1)}, f32[30,4096]{1,0:T(8,128)S(1)}, u32[]{:S(2)}, u32[]{:S(2)}) collective-permute-start(f32[30,4096]{1,0:T(8,128)S(1)} %collective-permute-done.2.refs_0_), channel_id=1, source_target_pairs={{0,8},{8,16},{16,24},{1,9},{9,17},{17,25},{2,10},{10,18},{18,26},{... | collective-permute-start | bytes 1474568 | tf_op jit(solution)/shard_map/ppermute | solution.py:164
  29.3 16.2 %collective-permute-start.5 = (f32[30,4096]{1,0:T(8,128)S(1)}, f32[30,4096]{1,0:T(8,128)S(1)}, u32[]{:S(2)}, u32[]{:S(2)}) collective-permute-start(f32[30,4096]{1,0:T(8,128)S(1)} %collective-permute-done.3.refs_1_), channel_id=1, source_target_pairs={{8,0},{16,8},{24,16},{9,1},{17,9},{25,17},{10,2},{18,10},{26,18},{... | collective-permute-start | bytes 1474568 | tf_op jit(solution)/shard_map/ppermute | solution.py:165
  41.4 16.2 %collective-permute-start.6 = (f32[30,4096]{1,0:T(8,128)S(1)}, f32[30,4096]{1,0:T(8,128)S(1)}, u32[]{:S(2)}, u32[]{:S(2)}) collective-permute-start(f32[30,4096]{1,0:T(8,128)S(1)} %collective-permute-done.4.refs_0_), channel_id=1, source_target_pairs={{0,8},{8,16},{16,24},{1,9},{9,17},{17,25},{2,10},{10,18},{18,26},{... | collective-permute-start | bytes 1474568 | tf_op jit(solution)/shard_map/ppermute | solution.py:164
  45.5 15.4 %collective-permute-start.7 = (f32[30,4096]{1,0:T(8,128)S(1)}, f32[30,4096]{1,0:T(8,128)S(1)}, u32[]{:S(2)}, u32[]{:S(2)}) collective-permute-start(f32[30,4096]{1,0:T(8,128)S(1)} %collective-permute-done.5.refs_1_), channel_id=1, source_target_pairs={{8,0},{16,8},{24,16},{9,1},{17,9},{25,17},{10,2},{18,10},{26,18},{... | collective-permute-start | bytes 1474568 | tf_op jit(solution)/shard_map/ppermute | solution.py:165
  71.7 1.2 %copy-start = (f32[24,64,256]{2,1,0:T(8,128)}, f32[24,64,256]{2,1,0:T(8,128)S(1)}, u32[]{:S(2)}) copy-start(f32[24,64,256]{2,1,0:T(8,128)S(1)} %shard_map.67.refs_3_) | copy-start | bytes 4718596
  90.2 6.2 %collective-permute-start.8 = (f32[30,512]{1,0:T(8,128)S(1)}, f32[30,512]{1,0:T(8,128)S(1)}, u32[]{:S(2)}, u32[]{:S(2)}) collective-permute-start(f32[30,512]{1,0:T(8,128)S(1)} %slice.44), channel_id=1, source_target_pairs={{0,1},{1,2},{2,3},{3,4},{4,5},{5,6},{6,7},{8,9},{9,10},{10,11},{11... | collective-permute-start | bytes 184328 | tf_op jit(solution)/shard_map/ppermute | solution.py:186
  96.5 6.2 %collective-permute-start.9 = (f32[30,512]{1,0:T(8,128)S(1)}, f32[30,512]{1,0:T(8,128)S(1)}, u32[]{:S(2)}, u32[]{:S(2)}) collective-permute-start(f32[30,512]{1,0:T(8,128)S(1)} %get-tuple-element.9), channel_id=1, source_target_pairs={{1,0},{2,1},{3,2},{4,3},{5,4},{6,5},{7,6},{9,8},{10,9},{11,10},{12... | collective-permute-start | bytes 184328 | tf_op jit(solution)/shard_map/ppermute | solution.py:185
